TPU v7x, 256 devices: a whole 4x4x8 slice. The times are simulated.
256 devices in a mesh: depth: 8 (over z_lo, y), lat: 32 (over z_hi, x, core).
Axes of the slice: x: 4, y: 4, z: 8 (z_hi: 4, z_lo: 2; z = z_hi * 2 + z_lo), core: 2. Of those that a mesh axis runs over, the one named last changes fastest.
Arguments:
- volume: float32 [64, 1024, 2048], P('depth', 'lat'), may hold values from 0.5 to 2
- measured: float32 [1024, 2048], P('lat'), may hold values from 0.2 to 2
- background: float32 [1024, 2048], P('lat'), may hold values from 0.1 to 1
- point_spread: float32 [64, 25, 25], P('depth'), may hold values from 2.5e-06 to 2.5e-05
Outputs:
- volume_next: float32 [64, 1024, 2048], P('depth', 'lat')
All inputs are finite; a program needn't handle non-finite values.
Results may differ from a plain program's by a relative error of at most 0.0001.
Values sent between devices are 32-bit elements; how exact they have to be, the bound alone decides.
A program may use at most 64 MiB of HBM per device.

v0:
```python
import jax
import jax.numpy as jnp
from jax import lax
from jax.experimental import pallas as pl
from jax.experimental.pallas import tpu as pltpu
from jax.sharding import PartitionSpec as P

ITERS = 2
WIDTH = 512
PAD = 32
MESH = pl.DeviceIdType.MESH
bf16, f32 = jnp.bfloat16, jnp.float32


def split(x):
    high = x.astype(bf16)
    return high, (x - high.astype(f32)).astype(bf16)


def dot3(x, w_high, w_low):
    x_high, x_low = split(x) if not isinstance(x, tuple) else x
    dot = lambda a, b: jnp.dot(a, b, preferred_element_type=f32)
    return dot(x_high, w_high[...]) + dot(x_low, w_high[...]) + dot(x_high, w_low[...])


def lanes(rows):
    return lax.broadcasted_iota(jnp.int32, (rows, 128), 1)


def quarters(rows, parts):
    lane = lanes(rows)
    first = jnp.where(lane < 32, parts[0], parts[1])
    return jnp.where(lane < 64, first, jnp.where(lane < 96, parts[2], parts[3]))


def tap_rows(point_spread):
    planes = point_spread.shape[0]
    taps = jnp.pad(point_spread[:, ::-1, :], ((0, 0), (0, 7), (0, 7)))
    return taps.reshape(planes, 32, 8, 4).transpose(3, 0, 2, 1).reshape(4 * planes, 256)


def build_weights(taps, work, fwd_high, fwd_low, adj_high, adj_low):
    rows = taps[...]
    sums = jnp.sum(rows, axis=1, keepdims=True)
    inverse = 1.0 / (sums[0:8] + sums[8:16] + sums[16:24] + sums[24:32])
    for jp in range(32):
        for half in range(2):
            block = jnp.broadcast_to(rows[jp : jp + 1, 128 * half : 128 * half + 128], (8, 128))
            work[8 * jp : 8 * jp + 8, 128 * half : 128 * half + 128] = pltpu.roll(
                block, 0, 1, stride=1, stride_axis=0
            )
    fwd_high[...], fwd_low[...] = split(work[...])
    for jp in range(32):
        p = jp % 8
        work[8 * jp : 8 * jp + 8, :] = work[8 * jp : 8 * jp + 8, :] * inverse[p : p + 1]
    adj_high[...], adj_low[...] = split(work[...].T)


def load_volume(volume, vt, vt_rolled, tile):
    cols = pl.ds(pl.multiple_of(tile * 128, 128), 128)
    rows = pl.ds(pl.multiple_of(tile * 128 + PAD, 8), 128)
    for a in range(2):
        block = jnp.concatenate(
            [volume[p, 8 * rb : 8 * rb + 8, cols] for rb in (2 * a, 2 * a + 1) for p in range(8)], 0
        ).T
        vt[a, rows, :] = block
        vt_rolled[a, rows, :] = pltpu.roll(block, 64, 1)


def forward(k, vt, vt_rolled, w_high, w_low, work, frame):
    rows = WIDTH + 32
    start = k * WIDTH
    lower = lanes(rows) < 64
    groups = [None] * 7
    for rb in range(4):
        a = rb // 2
        low, high = (vt, vt_rolled) if rb % 2 == 0 else (vt_rolled, vt)

        def pair(shift):
            return jnp.where(
                lower,
                low[a, pl.ds(start + 16 + shift, rows), :],
                high[a, pl.ds(start + 17 + shift, rows), :],
            )

        y = dot3(jnp.concatenate([pair(0), pair(2)], 1), w_high, w_low)
        work[rb, 0, 0 : WIDTH + 16, :] = y[: WIDTH + 16, :128] + y[16:, 128:]
        shifted = quarters(WIDTH, [work[rb, 0, o : o + WIDTH, :] for o in (4, 8, 12, 16)]).T
        for g in range(4):
            x = (shifted[8 * g : 8 * g + 8] + shifted[32 + 8 * g : 40 + 8 * g]) + (
                shifted[64 + 8 * g : 72 + 8 * g] + shifted[96 + 8 * g : 104 + 8 * g]
            )
            groups[rb + g] = x if groups[rb + g] is None else groups[rb + g] + x
    frame[4:60, :] = jnp.concatenate(groups, 0)


def load_ratio(ratio, qt, tile, inside):
    cols = pl.ds(pl.multiple_of(tile * 128, 128), 128)
    rows = pl.ds(pl.multiple_of(tile * 128 + PAD, 8), 128)
    x = jnp.where(inside, ratio[4:60, cols], 0.0)
    for rb in range(4):
        y = x[8 * rb : 8 * rb + 32]
        qt[rb, rows, :] = jnp.concatenate([y, y, y, y], 0).T


def adjoint(k, qt, w_high, w_low, work):
    rows = WIDTH + 32
    start = k * WIDTH
    lower = lanes(WIDTH) < 64
    sums = []
    for rb in range(4):
        x = quarters(rows, [qt[rb, pl.ds(start + o, rows), :] for o in (12, 8, 4, 0)])
        both = tuple(jnp.concatenate([h[16:], h[:-16]], 1) for h in split(x))
        z = dot3(both, w_high, w_low)
        work[rb, 0, 0 : WIDTH + 16, :] = z[:, :128]
        work[rb, 1, 0 : WIDTH + 16, :] = z[:, 128:]
        sums.append(
            jnp.where(
                lower,
                work[rb, 0, 16 : 16 + WIDTH, :] + work[rb, 1, 14 : 14 + WIDTH, :],
                work[rb, 0, 15 : 15 + WIDTH, :] + work[rb, 1, 13 : 13 + WIDTH, :],
            )
        )
    return [
        jnp.where(lower, x, y) + pltpu.roll(jnp.where(lower, y, x), 64, 1)
        for x, y in ((sums[0], sums[1]), (sums[2], sums[3]))
    ]


def kernel(
    n_depth, n_lat, chunks,
    volume, measured, background, taps, out,
    vt, vt_rolled, qt, work, w_work, fwd_high, fwd_low, adj_high, adj_low,
    frame, from_next, from_prev, centre, parts, own, ratio,
    halo_send, halo_recv, part_send, part_recv, gather_send, gather_recv, edge_send, edge_recv,
):
    depth, lat = lax.axis_index("depth"), lax.axis_index("lat")
    prev, following = lax.rem(lat + n_lat - 1, n_lat), lax.rem(lat + 1, n_lat)
    half = WIDTH // 2

    barrier = pltpu.get_barrier_semaphore()
    for o in range(1, n_depth):
        pl.semaphore_signal(
            barrier, inc=1, device_id=(lax.rem(depth + o, n_depth), lat), device_id_type=MESH
        )
    for neighbour in (prev, following):
        pl.semaphore_signal(barrier, inc=1, device_id=(depth, neighbour), device_id_type=MESH)

    def region(d, k, row, col):
        return (
            pl.ds(pl.multiple_of(row + 8 * lax.rem(d, 4), 8), 8),
            pl.ds(pl.multiple_of(col + half * (d // 4), half), half),
        )

    def remote(src, dst, send, recv, device):
        return pltpu.make_async_remote_copy(
            src_ref=src, dst_ref=dst, send_sem=send, recv_sem=recv, device_id=device, device_id_type=MESH
        )

    def halo_copies(it, k):
        n = it * chunks + k
        return [
            remote(frame.at[it, k, 0:16], from_next.at[it, k], halo_send.at[n, 0], halo_recv.at[n, 0], (depth, prev)),
            remote(frame.at[it, k, 48:64], from_prev.at[it, k], halo_send.at[n, 1], halo_recv.at[n, 1], (depth, following)),
        ]

    def part_copies(it, k):
        n = it * chunks + k
        copies = []
        for o in range(1, n_depth):
            owner = lax.rem(depth + o, n_depth)
            rows, cols = region(owner, k, 0, 0)
            copies.append(
                remote(centre.at[it, k, rows, cols], parts.at[it, k, o], part_send.at[n, o], part_recv.at[n, o], (owner, lat))
            )
        return copies

    def gather_copies(it, k):
        n = it * chunks + k
        rows, cols = region(depth, k, 16, k * WIDTH)
        return [
            remote(own.at[it, k], ratio.at[it, rows, cols], gather_send.at[n, o], gather_recv.at[n, o], (lax.rem(depth + o, n_depth), lat))
            for o in range(1, n_depth)
        ]

    def edge_copies(it, k):
        n = it * chunks + k
        cols = pl.ds(k * WIDTH, WIDTH)
        return [
            remote(ratio.at[it, 16:32, cols], ratio.at[it, 48:64, cols], edge_send.at[n, 0], edge_recv.at[n, 0], (depth, prev)),
            remote(ratio.at[it, 32:48, cols], ratio.at[it, 0:16, cols], edge_send.at[n, 1], edge_recv.at[n, 1], (depth, following)),
        ]

    def start(copies):
        for copy in copies:
            copy.start()

    def await_arrival(copies):
        for copy in copies:
            copy.wait_recv()

    def scatter_centre(it, k):
        await_arrival(halo_copies(it, k))
        centre[it, k, 0:16] = frame[it, k, 16:32] + jnp.where(lat > 0, from_prev[it, k], 0.0)
        centre[it, k, 16:32] = frame[it, k, 32:48] + jnp.where(lat < n_lat - 1, from_next[it, k], 0.0)
        start(part_copies(it, k))

    def divide(it, k):
        await_arrival(part_copies(it, k))
        rows, cols = region(depth, k, 0, 0)
        total = centre[it, k, rows, cols]
        for o in range(1, n_depth):
            total = total + parts[it, k, o]
        rows, cols = region(depth, k, 0, k * WIDTH)
        value = measured[rows, cols] / (total + background[rows, cols])
        own[it, k] = value
        rows, cols = region(depth, k, 16, k * WIDTH)
        ratio[it, rows, cols] = value
        start(gather_copies(it, k))

    def send_edges(it, k):
        await_arrival(gather_copies(it, k))
        start(edge_copies(it, k))

    frame_row = lax.broadcasted_iota(jnp.int32, (56, 128), 0)
    inside = ((frame_row >= 12) | (lat > 0)) & ((frame_row < 44) | (lat < n_lat - 1))

    def transpose_ratio(it, k):
        await_arrival(edge_copies(it, k))
        for t in range(WIDTH // 128):
            load_ratio(ratio.at[it], qt, k * (WIDTH // 128) + t, inside)

    def update(it, k):
        cols = pl.ds(k * WIDTH, WIDTH)
        rows = pl.ds(k * WIDTH + PAD, WIDTH)
        for a, factor in enumerate(adjoint(k, qt, adj_high, adj_low, work)):
            value = vt[a, rows, :] * factor
            if it < ITERS - 1:
                vt[a, rows, :] = value
                vt_rolled[a, rows, :] = pltpu.roll(value, 64, 1)
            else:
                block = value.T
                for i in range(16):
                    rb, p = 2 * a + i // 8, i % 8
                    out[p, 8 * rb : 8 * rb + 8, cols] = block[8 * i : 8 * i + 8]

    tail = vt.shape[1] - PAD - chunks * WIDTH
    for ref in (vt, vt_rolled, qt):
        ref[:, 0:PAD, :] = jnp.zeros((ref.shape[0], PAD, 128), f32)
        ref[:, PAD + chunks * WIDTH :, :] = jnp.zeros((ref.shape[0], tail, 128), f32)
    for it in range(ITERS):
        for k in range(chunks):
            frame[it, k, 0:8] = jnp.zeros((8, WIDTH), f32)
            frame[it, k, 56:64] = jnp.zeros((8, WIDTH), f32)
    build_weights(taps, w_work, fwd_high, fwd_low, adj_high, adj_low)

    def load_tiles(i, carry):
        for t in range(4):
            load_volume(volume, vt, vt_rolled, 4 * i + t)
        return carry

    lax.fori_loop(0, chunks * WIDTH // 512, load_tiles, 0)

    for it in range(ITERS):
        for k in range(chunks):
            forward(k, vt, vt_rolled, fwd_high, fwd_low, work, frame.at[it, k])
            if it == 0 and k == 0:
                pl.semaphore_wait(barrier, n_depth - 1 + 2)
            start(halo_copies(it, k))
            if k >= 2:
                scatter_centre(it, k - 2)
        scatter_centre(it, 2)
        divide(it, 0)
        scatter_centre(it, 3)
        divide(it, 1)
        send_edges(it, 0)
        divide(it, 2)
        send_edges(it, 1)
        divide(it, 3)
        send_edges(it, 2)
        transpose_ratio(it, 0)
        transpose_ratio(it, 1)
        send_edges(it, 3)
        update(it, 0)
        transpose_ratio(it, 2)
        update(it, 1)
        transpose_ratio(it, 3)
        update(it, 2)
        update(it, 3)

    for it in range(ITERS):
        for k in range(chunks):
            for copies in (halo_copies, part_copies, gather_copies, edge_copies):
                for copy in copies(it, k):
                    copy.wait_send()


def solution(mesh):
    n_depth, n_lat = mesh.shape["depth"], mesh.shape["lat"]

    def on_device(volume, measured, background, point_spread):
        planes, rows, cols = volume.shape
        chunks = cols // WIDTH
        steps = ITERS * chunks
        padded = cols + 2 * PAD
        vmem = lambda *shape, dtype=f32: pltpu.VMEM(shape, dtype)
        dma = lambda n: pltpu.SemaphoreType.DMA((steps, n))
        return pl.pallas_call(
            lambda *refs: kernel(n_depth, n_lat, chunks, *refs),
            out_shape=jax.ShapeDtypeStruct(volume.shape, f32),
            in_specs=[pl.BlockSpec(memory_space=pltpu.VMEM)] * 4,
            out_specs=pl.BlockSpec(memory_space=pltpu.VMEM),
            scratch_shapes=[
                vmem(2, padded, 128),
                vmem(2, padded, 128),
                vmem(4, padded, 128),
                vmem(4, 2, WIDTH + 32, 128),
                vmem(256, 256),
                vmem(256, 256, dtype=bf16),
                vmem(256, 256, dtype=bf16),
                vmem(256, 256, dtype=bf16),
                vmem(256, 256, dtype=bf16),
                vmem(ITERS, chunks, 64, WIDTH),
                vmem(ITERS, chunks, 16, WIDTH),
                vmem(ITERS, chunks, 16, WIDTH),
                vmem(ITERS, chunks, rows, WIDTH),
                vmem(ITERS, chunks, n_depth, 8, WIDTH // 2),
                vmem(ITERS, chunks, 8, WIDTH // 2),
                vmem(ITERS, 64, cols),
                dma(2), dma(2), dma(n_depth), dma(n_depth), dma(n_depth), dma(n_depth), dma(2), dma(2),
            ],
            compiler_params=pltpu.CompilerParams(
                collective_id=0, has_side_effects=True, vmem_limit_bytes=56 << 20
            ),
            cost_estimate=pl.CostEstimate(
                flops=2 * 3 * 4 * 4 * 2048 * 256 * 256, bytes_accessed=5 << 20, transcendentals=0
            ),
            name="deconvolve",
        )(volume, measured, background, tap_rows(point_spread))

    return jax.shard_map(
        on_device,
        mesh=mesh,
        in_specs=(P("depth", "lat", None), P("lat", None), P("lat", None), P("depth", None, None)),
        out_specs=P("depth", "lat", None),
        check_vma=False,
    )
```

profile of v0, /device:TPU:8, one launch (start us, length us, event | category | flops | bytes accessed | tf_op | source)
XLA Modules:
  0.0 75.2 jit_solution(17956642880051580982)
XLA Ops:
  0.0 1.0 %copy.6 = f32[8,25,25]{1,0,2:T(8,128)S(1)} copy(f32[8,25,25]{2,0,1:T(8,128)} %param.7) | data formatting | bytes 40000 | tf_op args[3]
  1.0 0.1 rev.3
  1.1 0.1 copy.7
  1.2 0.7 reshape.7.refs_3_
  1.9 70.1 %deconvolve.1 = f32[8,32,2048]{2,1,0:T(8,128)} custom-call(f32[8,32,2048]{2,1,0:T(8,128)} %refs_0_.1, f32[32,2048]{1,0:T(8,128)} %refs_1_.1, f32[32,2048]{1,0:T(8,128)} %refs_2_.1, f32[32,256]{1,0:T(8,128)} %reshape.7.refs_3_), custom_call_target="tpu_custom_call" | custom-call | flops 12884901888 | bytes 5242880 | tf_op jit(solution)/shard_map/deconvolve/pallas_call | solution.py:308
  72.1 3.1 %copy.9 = f32[8,32,2048]{2,1,0:T(8,128)} copy(f32[8,32,2048]{2,1,0:T(8,128)} %deconvolve.1) | data formatting | bytes 4194304
  (1 shorter events, 0.0 us)
where the time goes:
time: 75.4 us; the launch traced here: 75.2 us
  Pallas kernels  70.1 us (93%)
  local copies, waits for them, and re-layouts  5.05 us (7%)
    pallas_call x1, Pallas kernels, on_device(): pl.pallas_call(lambda *refs: kernel(n_depth, n_lat, chunks, *refs), out_s...  70.1 us
    unnamed x2, local copies, waits for them, and re-layouts  4.16 us

commit v1 on v0

v1 whole, which is shorter than its diff:
```python
import jax
import jax.numpy as jnp
from jax import lax
from jax.experimental import pallas as pl
from jax.experimental.pallas import tpu as pltpu
from jax.sharding import PartitionSpec as P

ITERS = 2
WIDTH = 512
PAD = 32
MESH = pl.DeviceIdType.MESH
bf16, f32 = jnp.bfloat16, jnp.float32


def split(x):
    high = x.astype(bf16)
    return high, (x - high.astype(f32)).astype(bf16)


def dot3(x, w_high, w_low):
    x_high, x_low = split(x) if not isinstance(x, tuple) else x
    dot = lambda a, b: jnp.dot(a, b, preferred_element_type=f32)
    return dot(x_high, w_high[...]) + dot(x_low, w_high[...]) + dot(x_high, w_low[...])


def lanes(rows):
    return lax.broadcasted_iota(jnp.int32, (rows, 128), 1)


def quarters(rows, parts):
    lane = lanes(rows)
    first = jnp.where(lane < 32, parts[0], parts[1])
    return jnp.where(lane < 64, first, jnp.where(lane < 96, parts[2], parts[3]))


def build_weights(point_spread, taps, work, fwd_high, fwd_low, adj_high, adj_low):
    count, planes, _ = point_spread.shape
    taps[...] = jnp.zeros_like(taps)
    for a in range(count):
        taps[8 * a : 8 * a + 8, 0:count] = point_spread[a]
    row = lax.broadcasted_iota(jnp.int32, (256, 256), 0)
    col = lax.broadcasted_iota(jnp.int32, (256, 256), 1)
    flip = (row % 8 == col // 32) & (row // 8 + col % 32 == count - 1)
    flipped = lax.dot_general(
        taps[:, 0:32], flip.astype(f32), (((0,), (0,)), ((), ())),
        precision=lax.Precision.HIGHEST, preferred_element_type=f32,
    )
    column_sums = jnp.sum(flipped, axis=0, keepdims=True)
    lane = lanes(8)
    for j in range(4):
        for p in range(planes):
            half = slice(128 * (p // 4), 128 * (p // 4) + 128)
            rows = slice(8 * (planes * j + p), 8 * (planes * j + p) + 8)
            for h in range(2):
                block = jnp.zeros((8, 128), f32)
                for g in range(4 * h, min(4 * h + 4, 7)):
                    source = jnp.broadcast_to(flipped[4 * g + j : 4 * g + j + 1, half], (8, 128))
                    moved = pltpu.roll(source, 32 * (g - p) % 128, 1, stride=1, stride_axis=0)
                    block = jnp.where(lane // 32 == g % 4, moved, block)
                work[rows, 128 * h : 128 * h + 128] = block
    fwd_high[...], fwd_low[...] = split(work[...])
    for p in range(planes):
        inverse = 1.0 / jnp.sum(column_sums[:, 32 * p : 32 * p + 32], axis=1, keepdims=True)
        for j in range(4):
            rows = slice(8 * (planes * j + p), 8 * (planes * j + p) + 8)
            work[rows, :] = work[rows, :] * inverse
    adj_high[...], adj_low[...] = split(work[...].T)


def load_volume(volume, vt, vt_rolled, tile):
    cols = pl.ds(pl.multiple_of(tile * 128, 128), 128)
    rows = pl.ds(pl.multiple_of(tile * 128 + PAD, 8), 128)
    for a in range(2):
        block = jnp.concatenate(
            [volume[p, 8 * rb : 8 * rb + 8, cols] for rb in (2 * a, 2 * a + 1) for p in range(8)], 0
        ).T
        vt[a, rows, :] = block
        vt_rolled[a, rows, :] = pltpu.roll(block, 64, 1)


def forward(k, vt, vt_rolled, w_high, w_low, work, frame):
    rows = WIDTH + 32
    start = k * WIDTH
    lower = lanes(rows) < 64
    groups = [None] * 7
    for rb in range(4):
        a = rb // 2
        low, high = (vt, vt_rolled) if rb % 2 == 0 else (vt_rolled, vt)

        def pair(shift):
            return jnp.where(
                lower,
                low[a, pl.ds(start + 16 + shift, rows), :],
                high[a, pl.ds(start + 17 + shift, rows), :],
            )

        y = dot3(jnp.concatenate([pair(0), pair(2)], 1), w_high, w_low)
        work[rb, 0, 0 : WIDTH + 16, :] = y[: WIDTH + 16, :128] + y[16:, 128:]
        shifted = quarters(WIDTH, [work[rb, 0, o : o + WIDTH, :] for o in (4, 8, 12, 16)]).T
        for g in range(4):
            x = (shifted[8 * g : 8 * g + 8] + shifted[32 + 8 * g : 40 + 8 * g]) + (
                shifted[64 + 8 * g : 72 + 8 * g] + shifted[96 + 8 * g : 104 + 8 * g]
            )
            groups[rb + g] = x if groups[rb + g] is None else groups[rb + g] + x
    frame[0:56, :] = jnp.concatenate(groups, 0)
    frame[56:64, :] = jnp.zeros((8, WIDTH), f32)


def load_ratio(ratio, qt, tile, inside):
    cols = pl.ds(pl.multiple_of(tile * 128, 128), 128)
    rows = pl.ds(pl.multiple_of(tile * 128 + PAD, 8), 128)
    x = jnp.where(inside, ratio[0:56, cols], 0.0)
    for rb in range(4):
        y = x[8 * rb : 8 * rb + 32]
        qt[rb, rows, :] = jnp.concatenate([y, y, y, y], 0).T


def adjoint(k, qt, w_high, w_low, work):
    rows = WIDTH + 32
    start = k * WIDTH
    lower = lanes(WIDTH) < 64
    sums = []
    for rb in range(4):
        x = quarters(rows, [qt[rb, pl.ds(start + o, rows), :] for o in (12, 8, 4, 0)])
        both = tuple(jnp.concatenate([h[16:], h[:-16]], 1) for h in split(x))
        z = dot3(both, w_high, w_low)
        work[rb, 0, 0 : WIDTH + 16, :] = z[:, :128]
        work[rb, 1, 0 : WIDTH + 16, :] = z[:, 128:]
        sums.append(
            jnp.where(
                lower,
                work[rb, 0, 16 : 16 + WIDTH, :] + work[rb, 1, 14 : 14 + WIDTH, :],
                work[rb, 0, 15 : 15 + WIDTH, :] + work[rb, 1, 13 : 13 + WIDTH, :],
            )
        )
    return [
        jnp.where(lower, x, y) + pltpu.roll(jnp.where(lower, y, x), 64, 1)
        for x, y in ((sums[0], sums[1]), (sums[2], sums[3]))
    ]


def kernel(
    n_depth, n_lat, chunks,
    volume_hbm, measured_hbm, background_hbm, point_spread, out_hbm,
    volume, vt, vt_rolled, qt, work, taps, w_work, fwd_high, fwd_low, adj_high, adj_low,
    frame, from_next, from_prev, total, parts, own, ratio, images, images_halo, mine, out,
    load_sem, image_sem, store_sem, image_send, image_recv, halo_send, halo_recv, part_send, part_recv, gather_send, gather_recv,
):
    depth, lat = lax.axis_index("depth"), lax.axis_index("lat")
    prev, following = lax.rem(lat + n_lat - 1, n_lat), lax.rem(lat + 1, n_lat)
    has_next, has_prev = lat < n_lat - 1, lat > 0

    barrier = pltpu.get_barrier_semaphore()
    for row in (prev, following):
        pl.semaphore_signal(barrier, inc=1, device_id=(depth, row), device_id_type=MESH)
    for o in range(1, n_depth):
        pl.semaphore_signal(
            barrier, inc=1, device_id=(lax.rem(depth + o, n_depth), lat), device_id_type=MESH
        )

    def columns(k):
        return pl.ds(k * WIDTH, WIDTH)

    def group(d):
        return pl.ds(pl.multiple_of(8 * d, 8), 8)

    def loads(k):
        return pltpu.make_async_copy(volume_hbm.at[:, :, columns(k)], volume.at[:, :, columns(k)], load_sem.at[k])

    def image_loads():
        return [
            pltpu.make_async_copy(image, images.at[i], image_sem.at[i])
            for i, image in enumerate((measured_hbm, background_hbm))
        ]

    def stores(k):
        return pltpu.make_async_copy(out.at[:, :, columns(k)], out_hbm.at[:, :, columns(k)], store_sem.at[k])

    for k in range(chunks):
        loads(k).start()
    for copy in image_loads():
        copy.start()

    def remote(src, dst, send, recv, device):
        return pltpu.make_async_remote_copy(
            src_ref=src, dst_ref=dst, send_sem=send, recv_sem=recv, device_id=device, device_id_type=MESH
        )

    def image_copies(rows, neighbour):
        return [
            remote(images.at[i, rows], images_halo.at[i], image_send.at[i], image_recv.at[i], (depth, neighbour))
            for i in range(2)
        ]

    needs_prev = depth <= 1
    needs_next = (depth == 5) | (depth == 6)

    def each_image(action):
        @pl.when(needs_prev)
        def _():
            for copy in image_copies(slice(16, 32), following):
                action(copy)

        @pl.when(needs_next)
        def _():
            for copy in image_copies(slice(0, 16), prev):
                action(copy)

    def gather_images():
        each_image(lambda copy: copy.wait_recv())
        for g in range(n_depth):

            @pl.when(depth == g)
            def _(g=g):
                for i in range(2):
                    if g == 0:
                        mine[i] = images_halo[i, 4:12]
                    elif g == 1:
                        mine[i, 0:4] = images_halo[i, 12:16]
                        mine[i, 4:8] = images[i, 0:4]
                    elif g == 5:
                        mine[i, 0:4] = images[i, 28:32]
                        mine[i, 4:8] = images_halo[i, 0:4]
                    elif g == 6:
                        mine[i] = images_halo[i, 4:12]
                    elif g == 7:
                        mine[i] = images[i, 0:8]
                    else:
                        mine[i] = images[i, 8 * g - 12 : 8 * g - 4]

    def halo_copy(it, k, up):
        n = it * chunks + k
        if up:
            return remote(frame.at[it, k, 0:24], from_next.at[it, k], halo_send.at[n, 0], halo_recv.at[n, 0], (depth, prev))
        return remote(frame.at[it, k, 32:56], from_prev.at[it, k], halo_send.at[n, 1], halo_recv.at[n, 1], (depth, following))

    def peer(o):
        return (lax.rem(depth + o, n_depth), lat)

    def part_copy(it, k, o):
        n = it * chunks + k
        owner, _ = peer(o)
        return remote(total.at[it, k, group(owner)], parts.at[it, k, o], part_send.at[n], part_recv.at[n], peer(o))

    def gather_copy(it, k, o):
        n = it * chunks + k
        return remote(own.at[it, k], ratio.at[it, group(depth), columns(k)], gather_send.at[n], gather_recv.at[n], peer(o))

    def all_of(it, k, send, recv):
        n = it * chunks + k
        every = parts.at[it, k, 1:n_depth]
        return remote(every, every, send.at[n], recv.at[n], peer(1))

    def halos(it, k, action):
        @pl.when(has_next)
        def _():
            action(halo_copy(it, k, False))

        @pl.when(has_prev)
        def _():
            action(halo_copy(it, k, True))

    def send_halos(it, k):
        halos(it, k, lambda copy: copy.start())

    def send_parts(it, k):
        total[it, k] = frame[it, k]

        @pl.when(has_prev)
        def _():
            halo_copy(it, k, False).wait_recv()
            total[it, k, 0:24] = total[it, k, 0:24] + from_prev[it, k]

        @pl.when(has_next)
        def _():
            halo_copy(it, k, True).wait_recv()
            total[it, k, 32:56] = total[it, k, 32:56] + from_next[it, k]

        for o in range(1, n_depth):
            part_copy(it, k, o).start()

    def await_part_sends(it, k):
        halos(it, k, lambda copy: copy.wait_send())
        all_of(it, k, part_send, part_recv).wait_send()

    def await_gather_sends(it, k):
        all_of(it, k, gather_send, gather_recv).wait_send()

    def divide(it, k):
        all_of(it, k, part_send, part_recv).wait_recv()
        rows = group(depth)
        value = total[it, k, rows]
        for o in range(1, n_depth):
            value = value + parts[it, k, o]
        value = mine[0, :, columns(k)] / (value + mine[1, :, columns(k)])
        own[it, k] = value
        for o in range(1, n_depth):
            gather_copy(it, k, o).start()
        ratio[it, rows, columns(k)] = value

    frame_row = lax.broadcasted_iota(jnp.int32, (56, 128), 0)
    inside = ((frame_row >= 12) | (lat > 0)) & ((frame_row < 44) | (lat < n_lat - 1))

    def await_ratio(it, k):
        all_of(it, k, gather_send, gather_recv).wait_recv()

    def transpose_ratio(it, k):
        for t in range(WIDTH // 128):
            load_ratio(ratio.at[it], qt, k * (WIDTH // 128) + t, inside)

    def update(it, k):
        rows = pl.ds(k * WIDTH + PAD, WIDTH)
        for a, factor in enumerate(adjoint(k, qt, adj_high, adj_low, work)):
            value = vt[a, rows, :] * factor
            if it < ITERS - 1:
                vt[a, rows, :] = value
                vt_rolled[a, rows, :] = pltpu.roll(value, 64, 1)
            else:
                block = value.T
                for i in range(16):
                    rb, p = 2 * a + i // 8, i % 8
                    out[p, 8 * rb : 8 * rb + 8, columns(k)] = block[8 * i : 8 * i + 8]
        if it == ITERS - 1:
            stores(k).start()

    build_weights(point_spread, taps, w_work, fwd_high, fwd_low, adj_high, adj_low)
    tail = vt.shape[1] - PAD - chunks * WIDTH
    for ref in (vt, vt_rolled, qt):
        ref[:, 0:PAD, :] = jnp.zeros((ref.shape[0], PAD, 128), f32)
        ref[:, PAD + chunks * WIDTH :, :] = jnp.zeros((ref.shape[0], tail, 128), f32)

    def transpose_volume(k):
        for t in range(WIDTH // 128):
            load_volume(volume, vt, vt_rolled, k * (WIDTH // 128) + t)

    for copy in image_loads():
        copy.wait()
    for k in range(chunks):
        loads(k).wait()
    for k in range(2):
        transpose_volume(k)

    for it in range(ITERS):
        for k in range(chunks):
            forward(k, vt, vt_rolled, fwd_high, fwd_low, work, frame.at[it, k])
            if it == 0 and k + 2 < chunks:
                transpose_volume(k + 2)
            if it == 0 and k == 0:
                pl.semaphore_wait(barrier, n_depth + 1)
            send_halos(it, k)
            if it == 0 and k == 0:
                each_image(lambda copy: copy.start())
            if k >= 2:
                send_parts(it, k - 2)
        for k in range(chunks - 2, chunks):
            send_parts(it, k)
        if it == 0:
            gather_images()
        else:
            for k in range(chunks):
                await_part_sends(it - 1, k)
                await_gather_sends(it - 1, k)
        for k in range(chunks):
            divide(it, k)
        if it == ITERS - 1:
            each_image(lambda copy: copy.wait_send())
            for k in range(chunks):
                await_part_sends(it, k)
        await_ratio(it, 0)
        transpose_ratio(it, 0)
        for k in range(chunks):
            if k + 1 < chunks:
                await_ratio(it, k + 1)
                transpose_ratio(it, k + 1)
            update(it, k)

    for k in range(chunks):
        await_gather_sends(ITERS - 1, k)
    for k in range(chunks):
        stores(k).wait()


def solution(mesh):
    n_depth, n_lat = mesh.shape["depth"], mesh.shape["lat"]

    def on_device(volume, measured, background, point_spread):
        planes, rows, cols = volume.shape
        chunks = cols // WIDTH
        steps = ITERS * chunks
        padded = cols + 2 * PAD
        vmem = lambda *shape, dtype=f32: pltpu.VMEM(shape, dtype)
        dma = lambda *shape: pltpu.SemaphoreType.DMA(shape)
        return pl.pallas_call(
            lambda *refs: kernel(n_depth, n_lat, chunks, *refs),
            out_shape=jax.ShapeDtypeStruct(volume.shape, f32),
            in_specs=[pl.BlockSpec(memory_space=pl.ANY)] * 3 + [pl.BlockSpec(memory_space=pltpu.VMEM)],
            out_specs=pl.BlockSpec(memory_space=pl.ANY),
            scratch_shapes=[
                vmem(planes, rows, cols),
                vmem(2, padded, 128),
                vmem(2, padded, 128),
                vmem(4, padded, 128),
                vmem(4, 2, WIDTH + 32, 128),
                vmem(256, 128),
                vmem(256, 256),
                vmem(256, 256, dtype=bf16),
                vmem(256, 256, dtype=bf16),
                vmem(256, 256, dtype=bf16),
                vmem(256, 256, dtype=bf16),
                vmem(ITERS, chunks, 64, WIDTH),
                vmem(ITERS, chunks, 24, WIDTH),
                vmem(ITERS, chunks, 24, WIDTH),
                vmem(ITERS, chunks, 64, WIDTH),
                vmem(ITERS, chunks, n_depth, 8, WIDTH),
                vmem(ITERS, chunks, 8, WIDTH),
                vmem(ITERS, 64, cols),
                vmem(2, rows, cols),
                vmem(2, 16, cols),
                vmem(2, 8, cols),
                vmem(planes, rows, cols),
                dma(chunks), dma(2), dma(chunks), dma(2), dma(2),
                dma(steps, 2), dma(steps, 2), dma(steps), dma(steps), dma(steps), dma(steps),
            ],
            compiler_params=pltpu.CompilerParams(
                collective_id=0, has_side_effects=True, vmem_limit_bytes=60 << 20
            ),
            cost_estimate=pl.CostEstimate(
                flops=2 * 3 * 4 * 4 * 2048 * 256 * 256, bytes_accessed=5 << 20, transcendentals=0
            ),
            name="deconvolve",
        )(volume, measured, background, point_spread.transpose(1, 0, 2))

    return jax.shard_map(
        on_device,
        mesh=mesh,
        in_specs=(P("depth", "lat", None), P("lat", None), P("lat", None), P("depth", None, None)),
        out_specs=P("depth", "lat", None),
        check_vma=False,
    )
```

time: 75.4 us -> 60.4 us (0.80)
  the two profiles are of different devices: /device:TPU:8 before, /device:TPU:71 now
where the time goes in v1:
time: 60.4 us; the launch traced here: 60.2 us
  Pallas kernels  57.1 us (95%)
  local copies, waits for them, and re-layouts  3.14 us (5%)
    pallas_call x1, Pallas kernels, on_device(): pl.pallas_call(lambda *refs: kernel(n_depth, n_lat, chunks, *refs), out_s...  57.1 us
    unnamed x1, local copies, waits for them, and re-layouts  3.14 us

profile of v1, /device:TPU:71, one launch (start us, length us, event | category | flops | bytes accessed | tf_op | source)
XLA Modules:
  0.0 60.2 jit_solution(16967774468968879792)
XLA Ops:
  0.0 57.1 %deconvolve.1 = f32[8,32,2048]{2,1,0:T(8,128)} custom-call(f32[8,32,2048]{2,1,0:T(8,128)} %refs_0_.1, f32[32,2048]{1,0:T(8,128)} %refs_1_.1, f32[32,2048]{1,0:T(8,128)} %refs_2_.1, f32[25,8,25]{2,1,0:T(8,128)} %bitcast.1), custom_call_target="tpu_custom_call" | custom-call | flops 12884901888 | bytes 5242880 | tf_op jit(solution)/shard_map/deconvolve/pallas_call | solution.py:393
  57.1 3.1 %copy.6 = f32[8,32,2048]{2,1,0:T(8,128)} copy(f32[8,32,2048]{2,1,0:T(8,128)} %deconvolve.1) | data formatting | bytes 4194304

commit v2 on v1

--- a/solution.py
+++ b/solution.py
@@ -115,22 +115,21 @@
         qt[rb, rows, :] = jnp.concatenate([y, y, y, y], 0).T
 
 
-def adjoint(k, qt, w_high, w_low, work):
-    rows = WIDTH + 32
-    start = k * WIDTH
-    lower = lanes(WIDTH) < 64
+def adjoint(start, width, qt, w_high, w_low, work):
+    rows = width + 32
+    lower = lanes(width) < 64
     sums = []
     for rb in range(4):
         x = quarters(rows, [qt[rb, pl.ds(start + o, rows), :] for o in (12, 8, 4, 0)])
         both = tuple(jnp.concatenate([h[16:], h[:-16]], 1) for h in split(x))
         z = dot3(both, w_high, w_low)
-        work[rb, 0, 0 : WIDTH + 16, :] = z[:, :128]
-        work[rb, 1, 0 : WIDTH + 16, :] = z[:, 128:]
+        work[rb, 0, 0 : width + 16, :] = z[:, :128]
+        work[rb, 1, 0 : width + 16, :] = z[:, 128:]
         sums.append(
             jnp.where(
                 lower,
-                work[rb, 0, 16 : 16 + WIDTH, :] + work[rb, 1, 14 : 14 + WIDTH, :],
-                work[rb, 0, 15 : 15 + WIDTH, :] + work[rb, 1, 13 : 13 + WIDTH, :],
+                work[rb, 0, 16 : 16 + width, :] + work[rb, 1, 14 : 14 + width, :],
+                work[rb, 0, 15 : 15 + width, :] + work[rb, 1, 13 : 13 + width, :],
             )
         )
     return [
@@ -143,7 +142,7 @@
     n_depth, n_lat, chunks,
     volume_hbm, measured_hbm, background_hbm, point_spread, out_hbm,
     volume, vt, vt_rolled, qt, work, taps, w_work, fwd_high, fwd_low, adj_high, adj_low,
-    frame, from_next, from_prev, total, parts, own, ratio, images, images_halo, mine, out,
+    frame, from_next, from_prev, total, parts, own, ratio, images, images_edge, images_halo, mine, out,
     load_sem, image_sem, store_sem, image_send, image_recv, halo_send, halo_recv, part_send, part_recv, gather_send, gather_recv,
 ):
     depth, lat = lax.axis_index("depth"), lax.axis_index("lat")
@@ -174,7 +173,9 @@
         ]
 
     def stores(k):
-        return pltpu.make_async_copy(out.at[:, :, columns(k)], out_hbm.at[:, :, columns(k)], store_sem.at[k])
+        first, end = store_range(k)
+        cols = pl.ds(first, end - first)
+        return pltpu.make_async_copy(out.at[:, :, cols], out_hbm.at[:, :, cols], store_sem.at[k])
 
     for k in range(chunks):
         loads(k).start()
@@ -186,25 +187,29 @@
             src_ref=src, dst_ref=dst, send_sem=send, recv_sem=recv, device_id=device, device_id_type=MESH
         )
 
-    def image_copies(rows, neighbour):
-        return [
-            remote(images.at[i, rows], images_halo.at[i], image_send.at[i], image_recv.at[i], (depth, neighbour))
-            for i in range(2)
-        ]
-
-    needs_prev = depth <= 1
-    needs_next = (depth == 5) | (depth == 6)
-
     def each_image(action):
-        @pl.when(needs_prev)
-        def _():
-            for copy in image_copies(slice(16, 32), following):
-                action(copy)
-
-        @pl.when(needs_next)
-        def _():
-            for copy in image_copies(slice(0, 16), prev):
-                action(copy)
+        for g, count, neighbour in ((0, 2, following), (1, 1, following), (5, 1, prev), (6, 2, prev)):
+
+            @pl.when(depth == g)
+            def _(count=count, neighbour=neighbour):
+                action(
+                    remote(
+                        images_edge.at[0:count], images_halo.at[0:count],
+                        image_send, image_recv, (depth, neighbour),
+                    )
+                )
+
+    def pack_images():
+        for g, first, count in ((0, 20, 8), (1, 28, 4), (5, 0, 4), (6, 4, 8)):
+
+            @pl.when(depth == g)
+            def _(first=first, count=count):
+                for i in range(2):
+                    rows = images[i, first : first + count]
+                    if count == 8:
+                        images_edge[i] = rows
+                    else:
+                        images_edge[0, 4 * i : 4 * i + 4] = rows
 
     def gather_images():
         each_image(lambda copy: copy.wait_recv())
@@ -213,16 +218,14 @@
             @pl.when(depth == g)
             def _(g=g):
                 for i in range(2):
-                    if g == 0:
-                        mine[i] = images_halo[i, 4:12]
+                    if g in (0, 6):
+                        mine[i] = images_halo[i]
                     elif g == 1:
-                        mine[i, 0:4] = images_halo[i, 12:16]
+                        mine[i, 0:4] = images_halo[0, 4 * i : 4 * i + 4]
                         mine[i, 4:8] = images[i, 0:4]
                     elif g == 5:
                         mine[i, 0:4] = images[i, 28:32]
-                        mine[i, 4:8] = images_halo[i, 0:4]
-                    elif g == 6:
-                        mine[i] = images_halo[i, 4:12]
+                        mine[i, 4:8] = images_halo[0, 4 * i : 4 * i + 4]
                     elif g == 7:
                         mine[i] = images[i, 0:8]
                     else:
@@ -308,19 +311,28 @@
         for t in range(WIDTH // 128):
             load_ratio(ratio.at[it], qt, k * (WIDTH // 128) + t, inside)
 
+    def update_range(k):
+        return max(k * WIDTH - 16, 0), (k + 1) * WIDTH - (16 if k + 1 < chunks else 0)
+
+    def store_range(k):
+        first, end = update_range(k)
+        return first // 128 * 128, end // 128 * 128
+
     def update(it, k):
-        rows = pl.ds(k * WIDTH + PAD, WIDTH)
-        for a, factor in enumerate(adjoint(k, qt, adj_high, adj_low, work)):
+        first, end = update_range(k)
+        rows = pl.ds(first + PAD, end - first)
+        for a, factor in enumerate(adjoint(first, end - first, qt, adj_high, adj_low, work)):
             value = vt[a, rows, :] * factor
+            vt[a, rows, :] = value
             if it < ITERS - 1:
-                vt[a, rows, :] = value
                 vt_rolled[a, rows, :] = pltpu.roll(value, 64, 1)
-            else:
-                block = value.T
+        if it == ITERS - 1:
+            first, end = store_range(k)
+            for a in range(2):
+                block = vt[a, first + PAD : end + PAD, :].T
                 for i in range(16):
                     rb, p = 2 * a + i // 8, i % 8
-                    out[p, 8 * rb : 8 * rb + 8, columns(k)] = block[8 * i : 8 * i + 8]
-        if it == ITERS - 1:
+                    out[p, 8 * rb : 8 * rb + 8, first:end] = block[8 * i : 8 * i + 8]
             stores(k).start()
 
     build_weights(point_spread, taps, w_work, fwd_high, fwd_low, adj_high, adj_low)
@@ -335,45 +347,55 @@
 
     for copy in image_loads():
         copy.wait()
+    pack_images()
     for k in range(chunks):
         loads(k).wait()
     for k in range(2):
         transpose_volume(k)
 
+    def predict(it, k):
+        forward(k, vt, vt_rolled, fwd_high, fwd_low, work, frame.at[it, k])
+
+    last = chunks - 1
+    for k in range(chunks):
+        predict(0, k)
+        if k + 2 < chunks:
+            transpose_volume(k + 2)
+        if k == 0:
+            pl.semaphore_wait(barrier, n_depth + 1)
+            each_image(lambda copy: copy.start())
+        send_halos(0, k)
+    for k in range(chunks):
+        send_parts(0, k)
+    gather_images()
+
     for it in range(ITERS):
         for k in range(chunks):
-            forward(k, vt, vt_rolled, fwd_high, fwd_low, work, frame.at[it, k])
-            if it == 0 and k + 2 < chunks:
-                transpose_volume(k + 2)
-            if it == 0 and k == 0:
-                pl.semaphore_wait(barrier, n_depth + 1)
-            send_halos(it, k)
-            if it == 0 and k == 0:
-                each_image(lambda copy: copy.start())
-            if k >= 2:
-                send_parts(it, k - 2)
-        for k in range(chunks - 2, chunks):
-            send_parts(it, k)
-        if it == 0:
-            gather_images()
-        else:
-            for k in range(chunks):
-                await_part_sends(it - 1, k)
-                await_gather_sends(it - 1, k)
+            if it == 0 or k > 1:
+                divide(it, k)
         for k in range(chunks):
-            divide(it, k)
-        if it == ITERS - 1:
-            each_image(lambda copy: copy.wait_send())
+            await_ratio(it, k)
+            transpose_ratio(it, k)
+            update(it, k)
+            if it < ITERS - 1 and k > 0:
+                predict(it + 1, k - 1)
+                send_halos(it + 1, k - 1)
+        if it < ITERS - 1:
+            send_parts(it + 1, 0)
+            predict(it + 1, last)
+            send_halos(it + 1, last)
+            send_parts(it + 1, 1)
+            divide(it + 1, 0)
+            send_parts(it + 1, 2)
+            send_parts(it + 1, 3)
+            divide(it + 1, 1)
             for k in range(chunks):
                 await_part_sends(it, k)
-        await_ratio(it, 0)
-        transpose_ratio(it, 0)
-        for k in range(chunks):
-            if k + 1 < chunks:
-                await_ratio(it, k + 1)
-                transpose_ratio(it, k + 1)
-            update(it, k)
-
+                await_gather_sends(it, k)
+
+    each_image(lambda copy: copy.wait_send())
+    for k in range(chunks):
+        await_part_sends(ITERS - 1, k)
     for k in range(chunks):
         await_gather_sends(ITERS - 1, k)
     for k in range(chunks):
@@ -415,10 +437,11 @@
                 vmem(ITERS, chunks, 8, WIDTH),
                 vmem(ITERS, 64, cols),
                 vmem(2, rows, cols),
-                vmem(2, 16, cols),
+                vmem(2, 8, cols),
+                vmem(2, 8, cols),
                 vmem(2, 8, cols),
                 vmem(planes, rows, cols),
-                dma(chunks), dma(2), dma(chunks), dma(2), dma(2),
+                dma(chunks), dma(2), dma(chunks), pltpu.SemaphoreType.DMA, pltpu.SemaphoreType.DMA,
                 dma(steps, 2), dma(steps, 2), dma(steps), dma(steps), dma(steps), dma(steps),
             ],
             compiler_params=pltpu.CompilerParams(

time: 60.4 us -> 55.2 us (0.914)
  the two profiles are of different devices: /device:TPU:71 before, /device:TPU:8 now
where the time goes in v2:
time: 55.2 us; the launch traced here: 55 us
  Pallas kernels  51.9 us (94%)
  local copies, waits for them, and re-layouts  3.14 us (6%)
    pallas_call x1, Pallas kernels, on_device(): pl.pallas_call(lambda *refs: kernel(n_depth, n_lat, chunks, *refs), out_s...  51.9 us
    unnamed x1, local copies, waits for them, and re-layouts  3.14 us

profile of v2, /device:TPU:8, one launch (start us, length us, event | category | flops | bytes accessed | tf_op | source)
XLA Modules:
  0.0 55.0 jit_solution(3897423887195326584)
XLA Ops:
  0.0 51.9 %deconvolve.1 = f32[8,32,2048]{2,1,0:T(8,128)} custom-call(f32[8,32,2048]{2,1,0:T(8,128)} %refs_0_.1, f32[32,2048]{1,0:T(8,128)} %refs_1_.1, f32[32,2048]{1,0:T(8,128)} %refs_2_.1, f32[25,8,25]{2,1,0:T(8,128)} %bitcast.1), custom_call_target="tpu_custom_call" | custom-call | flops 12884901888 | bytes 5242880 | tf_op jit(solution)/shard_map/deconvolve/pallas_call | solution.py:415
  51.9 3.1 %copy.6 = f32[8,32,2048]{2,1,0:T(8,128)} copy(f32[8,32,2048]{2,1,0:T(8,128)} %deconvolve.1) | data formatting | bytes 4194304

commit v3 on v2

--- a/solution.py
+++ b/solution.py
@@ -106,20 +106,21 @@
     frame[56:64, :] = jnp.zeros((8, WIDTH), f32)
 
 
-def load_ratio(ratio, qt, tile, inside):
+def load_ratio(ratio, qt, tile, inside, rbs):
     cols = pl.ds(pl.multiple_of(tile * 128, 128), 128)
     rows = pl.ds(pl.multiple_of(tile * 128 + PAD, 8), 128)
     x = jnp.where(inside, ratio[0:56, cols], 0.0)
-    for rb in range(4):
+    for rb in rbs:
         y = x[8 * rb : 8 * rb + 32]
         qt[rb, rows, :] = jnp.concatenate([y, y, y, y], 0).T
 
 
-def adjoint(start, width, qt, w_high, w_low, work):
+def adjoint(start, width, qt, w_high, w_low, work, prepare):
     rows = width + 32
     lower = lanes(width) < 64
     sums = []
     for rb in range(4):
+        prepare(rb)
         x = quarters(rows, [qt[rb, pl.ds(start + o, rows), :] for o in (12, 8, 4, 0)])
         both = tuple(jnp.concatenate([h[16:], h[:-16]], 1) for h in split(x))
         z = dot3(both, w_high, w_low)
@@ -140,10 +141,10 @@
 
 def kernel(
     n_depth, n_lat, chunks,
-    volume_hbm, measured_hbm, background_hbm, point_spread, out_hbm,
-    volume, vt, vt_rolled, qt, work, taps, w_work, fwd_high, fwd_low, adj_high, adj_low,
+    volume_hbm, measured_hbm, background_hbm, point_spread_hbm, out_hbm,
+    volume, point_spread, vt, vt_rolled, qt, work, taps, w_work, fwd_high, fwd_low, adj_high, adj_low,
     frame, from_next, from_prev, total, parts, own, ratio, images, images_edge, images_halo, mine, out,
-    load_sem, image_sem, store_sem, image_send, image_recv, halo_send, halo_recv, part_send, part_recv, gather_send, gather_recv,
+    load_sem, taps_sem, image_sem, store_sem, image_send, image_recv, halo_send, halo_recv, part_send, part_recv, gather_send, gather_recv,
 ):
     depth, lat = lax.axis_index("depth"), lax.axis_index("lat")
     prev, following = lax.rem(lat + n_lat - 1, n_lat), lax.rem(lat + 1, n_lat)
@@ -177,6 +178,8 @@
         cols = pl.ds(first, end - first)
         return pltpu.make_async_copy(out.at[:, :, cols], out_hbm.at[:, :, cols], store_sem.at[k])
 
+    taps_load = pltpu.make_async_copy(point_spread_hbm, point_spread, taps_sem)
+    taps_load.start()
     for k in range(chunks):
         loads(k).start()
     for copy in image_loads():
@@ -272,12 +275,12 @@
         @pl.when(has_prev)
         def _():
             halo_copy(it, k, False).wait_recv()
-            total[it, k, 0:24] = total[it, k, 0:24] + from_prev[it, k]
+            total[it, k, 0:24] = frame[it, k, 0:24] + from_prev[it, k]
 
         @pl.when(has_next)
         def _():
             halo_copy(it, k, True).wait_recv()
-            total[it, k, 32:56] = total[it, k, 32:56] + from_next[it, k]
+            total[it, k, 32:56] = frame[it, k, 32:56] + from_next[it, k]
 
         for o in range(1, n_depth):
             part_copy(it, k, o).start()
@@ -307,9 +310,9 @@
     def await_ratio(it, k):
         all_of(it, k, gather_send, gather_recv).wait_recv()
 
-    def transpose_ratio(it, k):
+    def transpose_ratio(it, k, rb):
         for t in range(WIDTH // 128):
-            load_ratio(ratio.at[it], qt, k * (WIDTH // 128) + t, inside)
+            load_ratio(ratio.at[it], qt, k * (WIDTH // 128) + t, inside, (rb,))
 
     def update_range(k):
         return max(k * WIDTH - 16, 0), (k + 1) * WIDTH - (16 if k + 1 < chunks else 0)
@@ -321,7 +324,7 @@
     def update(it, k):
         first, end = update_range(k)
         rows = pl.ds(first + PAD, end - first)
-        for a, factor in enumerate(adjoint(first, end - first, qt, adj_high, adj_low, work)):
+        for a, factor in enumerate(adjoint(first, end - first, qt, adj_high, adj_low, work, lambda rb: transpose_ratio(it, k, rb))):
             value = vt[a, rows, :] * factor
             vt[a, rows, :] = value
             if it < ITERS - 1:
@@ -335,6 +338,7 @@
                     out[p, 8 * rb : 8 * rb + 8, first:end] = block[8 * i : 8 * i + 8]
             stores(k).start()
 
+    taps_load.wait()
     build_weights(point_spread, taps, w_work, fwd_high, fwd_low, adj_high, adj_low)
     tail = vt.shape[1] - PAD - chunks * WIDTH
     for ref in (vt, vt_rolled, qt):
@@ -375,7 +379,6 @@
                 divide(it, k)
         for k in range(chunks):
             await_ratio(it, k)
-            transpose_ratio(it, k)
             update(it, k)
             if it < ITERS - 1 and k > 0:
                 predict(it + 1, k - 1)
@@ -415,10 +418,11 @@
         return pl.pallas_call(
             lambda *refs: kernel(n_depth, n_lat, chunks, *refs),
             out_shape=jax.ShapeDtypeStruct(volume.shape, f32),
-            in_specs=[pl.BlockSpec(memory_space=pl.ANY)] * 3 + [pl.BlockSpec(memory_space=pltpu.VMEM)],
+            in_specs=[pl.BlockSpec(memory_space=pl.ANY)] * 4,
             out_specs=pl.BlockSpec(memory_space=pl.ANY),
             scratch_shapes=[
                 vmem(planes, rows, cols),
+                vmem(point_spread.shape[1], planes, point_spread.shape[2]),
                 vmem(2, padded, 128),
                 vmem(2, padded, 128),
                 vmem(4, padded, 128),
@@ -441,7 +445,7 @@
                 vmem(2, 8, cols),
                 vmem(2, 8, cols),
                 vmem(planes, rows, cols),
-                dma(chunks), dma(2), dma(chunks), pltpu.SemaphoreType.DMA, pltpu.SemaphoreType.DMA,
+                dma(chunks), pltpu.SemaphoreType.DMA, dma(2), dma(chunks), pltpu.SemaphoreType.DMA, pltpu.SemaphoreType.DMA,
                 dma(steps, 2), dma(steps, 2), dma(steps), dma(steps), dma(steps), dma(steps),
             ],
             compiler_params=pltpu.CompilerParams(

time: 55.2 us -> 54.4 us (0.986); the launches traced: 55 us -> 53.6 us
  Pallas kernels: 51.9 us -> 50.5 us
    pallas_call x1, Pallas kernels: 51.9 us -> 50.5 us  [on_device(): pl.pallas_call(lambda *refs: kernel(n_depth, n_lat, chunks, *refs), out_s...]
where the time goes in v3:
time: 54.4 us; the launch traced here: 53.6 us
  Pallas kernels  50.5 us (93%)
  local copies, waits for them, and re-layouts  3.14 us (6%)
    pallas_call x1, Pallas kernels, on_device(): pl.pallas_call(lambda *refs: kernel(n_depth, n_lat, chunks, *refs), out_s...  50.5 us
    unnamed x1, local copies, waits for them, and re-layouts  3.14 us

profile of v3, /device:TPU:8, one launch (start us, length us, event | category | flops | bytes accessed | tf_op | source)
XLA Modules:
  0.0 53.6 jit_solution(4125132057937762227)
XLA Ops:
  0.0 50.5 %deconvolve.1 = f32[8,32,2048]{2,1,0:T(8,128)} custom-call(f32[8,32,2048]{2,1,0:T(8,128)} %refs_0_.1, f32[32,2048]{1,0:T(8,128)} %refs_1_.1, f32[32,2048]{1,0:T(8,128)} %refs_2_.1, f32[25,8,25]{2,1,0:T(8,128)} %bitcast.1), custom_call_target="tpu_custom_call" | custom-call | flops 12884901888 | bytes 5242880 | tf_op jit(solution)/shard_map/deconvolve/pallas_call | solution.py:418
  50.5 3.1 %copy.6 = f32[8,32,2048]{2,1,0:T(8,128)} copy(f32[8,32,2048]{2,1,0:T(8,128)} %deconvolve.1) | data formatting | bytes 4194304

commit v4 on v3

--- a/solution.py
+++ b/solution.py
@@ -240,6 +240,8 @@
             return remote(frame.at[it, k, 0:24], from_next.at[it, k], halo_send.at[n, 0], halo_recv.at[n, 0], (depth, prev))
         return remote(frame.at[it, k, 32:56], from_prev.at[it, k], halo_send.at[n, 1], halo_recv.at[n, 1], (depth, following))
 
+    farthest_first = sorted(range(1, n_depth), key=lambda o: -min(o % 4, 4 - o % 4))
+
     def peer(o):
         return (lax.rem(depth + o, n_depth), lat)
 
@@ -282,7 +284,7 @@
             halo_copy(it, k, True).wait_recv()
             total[it, k, 32:56] = frame[it, k, 32:56] + from_next[it, k]
 
-        for o in range(1, n_depth):
+        for o in farthest_first:
             part_copy(it, k, o).start()
 
     def await_part_sends(it, k):
@@ -300,7 +302,7 @@
             value = value + parts[it, k, o]
         value = mine[0, :, columns(k)] / (value + mine[1, :, columns(k)])
         own[it, k] = value
-        for o in range(1, n_depth):
+        for o in farthest_first:
             gather_copy(it, k, o).start()
         ratio[it, rows, columns(k)] = value
 

time: 54.4 us -> 53.7 us (0.987)
  Pallas kernels: 50.5 us -> 49.7 us
    pallas_call x1, Pallas kernels: 50.5 us -> 49.7 us  [on_device(): pl.pallas_call(lambda *refs: kernel(n_depth, n_lat, chunks, *refs), out_s...]
where the time goes in v4:
time: 53.7 us; the launch traced here: 52.9 us
  Pallas kernels  49.7 us (93%)
  local copies, waits for them, and re-layouts  3.14 us (6%)
    pallas_call x1, Pallas kernels, on_device(): pl.pallas_call(lambda *refs: kernel(n_depth, n_lat, chunks, *refs), out_s...  49.7 us
    unnamed x1, local copies, waits for them, and re-layouts  3.14 us

profile of v4, /device:TPU:8, one launch (start us, length us, event | category | flops | bytes accessed | tf_op | source)
XLA Modules:
  0.0 52.9 jit_solution(2120718252705264963)
XLA Ops:
  0.0 49.7 %deconvolve.1 = f32[8,32,2048]{2,1,0:T(8,128)} custom-call(f32[8,32,2048]{2,1,0:T(8,128)} %refs_0_.1, f32[32,2048]{1,0:T(8,128)} %refs_1_.1, f32[32,2048]{1,0:T(8,128)} %refs_2_.1, f32[25,8,25]{2,1,0:T(8,128)} %bitcast.1), custom_call_target="tpu_custom_call" | custom-call | flops 12884901888 | bytes 5242880 | tf_op jit(solution)/shard_map/deconvolve/pallas_call | solution.py:420
  49.7 3.1 %copy.6 = f32[8,32,2048]{2,1,0:T(8,128)} copy(f32[8,32,2048]{2,1,0:T(8,128)} %deconvolve.1) | data formatting | bytes 4194304
